TPU v7x, 32 devices: a whole 2x2x4 slice. The times are simulated.
32 devices in a mesh: seq: 8 (over z, y), head: 4 (over x, core).
Axes of the slice: x: 2, y: 2, z: 4, core: 2. Of those that a mesh axis runs over, the one named last changes fastest.
Arguments:
- mamba_inner: bfloat16 [1024, 3072], P('seq', 'head'), may hold values from -6 to 6
- mamba_groups: bfloat16 [1024, 512], P('seq'), may hold values from -6 to 6
- selective_gate: bfloat16 [1024, 3072], P('seq', 'head'), may hold values from -6 to 6
- step_raw: float32 [48, 1024], P('head', 'seq'), may hold values from -3 to 3
- step_bias: float32 [48], P('head'), may hold values from -0.5 to 0.5
- decay_log: float32 [48], P('head'), may hold values from -12 to -2
- conv_inner: float32 [4, 3072], P(None, 'head'), may hold values from -3 to 3
- conv_groups: float32 [4, 512], replicated, may hold values from -3 to 3
- gated_norm_gain: float32 [3072], P('head'), may hold values from 0.1 to 1.9
- query_rows: bfloat16 [1024, 1024], P('seq', 'head'), may hold values from -8 to 8
- key_rows: bfloat16 [1024, 256], P('seq'), may hold values from -8 to 8
- value_rows: bfloat16 [1024, 256], P('seq'), may hold values from -6 to 6
- segment_ids: int32 [1024], P('seq'), may hold values from 0 to 15, never falling along the last dimension, each value on 1 to 682 neighbouring positions
- mamba_proj: bfloat16 [3072, 2048], P('head'), may hold values from -0.109375 to 0.109375
- attn_proj: bfloat16 [1024, 2048], P('head'), may hold values from -0.1875 to 0.1875
Outputs:
- mixed: bfloat16 [1024, 2048], P('seq', 'head')
Inputs may be any that keep to these rules, and one draw needn't show every extreme that they name: `segment_ids`: prompt numbers never fall along the tokens; each prompt holds 1 to 682 tokens and one holds exactly 682.
All inputs are finite; a program needn't handle non-finite values.
Results may differ from a plain program's by a relative error of at most 0.015.
Values may be sent and summed in bfloat16 or wider, within the bound.
A program may use at most 128 MiB of HBM per device.

v0:
```python
import math
import jax
import jax.numpy as jnp
from jax import lax
from jax.sharding import PartitionSpec as P

HEAD_CHANNELS = 64
STATE_SIZE = 256
QH = 8
KVH = 2
HD = 128


def shifted(value, axis, steps):
    count = lax.axis_size(axis)
    first, last = (max(0, -steps), min(count, count - steps))
    return lax.ppermute(value, axis, [(source, source + steps) for source in range(first, last)])


def entering(array, axis, combine, identity):
    length, position = (lax.axis_size(axis), lax.axis_index(axis))
    everything = jax.tree.map(
        lambda part, kind: lax.all_gather(part.astype(kind), axis),
        array,
        (jnp.bfloat16, jnp.bfloat16),
    )
    start = jax.tree.map(
        lambda part, zero: jnp.broadcast_to(jnp.asarray(zero, part.dtype), part.shape),
        array,
        identity,
    )

    def turn(k, before):
        reached = k < position
        new = combine(
            before, jax.tree.map(lambda part, own: part[k].astype(own.dtype), everything, array)
        )
        return jax.tree.map(lambda a, b: jnp.where(reached, a, b), new, before)

    return lax.fori_loop(0, length, turn, start)


def conv_silu(rows, weight, segs, rim_rows, rim_segs):
    item_count = rows.shape[0]
    padded = jnp.concatenate([rim_rows.astype(jnp.float32), rows.astype(jnp.float32)], 0)
    seg_pad = jnp.concatenate([rim_segs, segs], 0)
    total = jnp.zeros(rows.shape, jnp.float32)
    for offset in range(weight.shape[0]):
        window = padded[offset : offset + item_count]
        keep = (seg_pad[offset : offset + item_count] == segs).astype(jnp.float32)
        total = total + weight[offset][None, :] * window * keep[:, None]
    return jax.nn.silu(total).astype(jnp.bfloat16)


def mamba_local(inner, groups, segs, steps, rates, prev_last):
    highest = lax.Precision.HIGHEST
    cumul = jnp.cumsum(-steps * rates[:, None], axis=1)
    read_b = groups[:, :STATE_SIZE]
    read_c = groups[:, STATE_SIZE:]
    intersection = jnp.dot(read_c, read_b.T, preferred_element_type=jnp.float32)
    order = jnp.arange(segs.shape[0], dtype=jnp.int32)
    live = (segs[:, None] == segs[None, :]) & (order[:, None] >= order[None, :])
    decays = jnp.exp(jnp.where(live[None], cumul[:, :, None] - cumul[:, None, :], -jnp.inf))
    mixing = intersection[None] * decays
    scaled = inner.astype(jnp.float32) * steps.T[:, :, None]
    output = jnp.einsum("htj,jhd->thd", mixing, scaled, precision=highest)
    tail = jnp.exp(cumul[:, -1:] - cumul) * (segs == segs[-1]).astype(jnp.float32)[None, :]
    local_state = jnp.einsum(
        "ht,thd,tn->hdn", tail, scaled, read_b.astype(jnp.float32), precision=highest
    )
    through = jnp.exp(cumul[:, -1]) * (segs[-1] == prev_last).astype(jnp.float32)
    return (output, through, local_state, cumul)


def mamba_incoming(output, incoming, groups, segs, cumul, prev_last):
    read_c = groups[:, STATE_SIZE:].astype(jnp.float32)
    joined = (segs == prev_last).astype(jnp.float32)
    from_carry = jnp.einsum("hdn,tn->thd", incoming, read_c, precision=lax.Precision.HIGHEST)
    return output + jnp.exp(cumul).T[:, :, None] * joined[:, None, None] * from_carry


def combine_states(earlier, later):
    return (earlier[0] * later[0], later[0][:, None, None] * earlier[1] + later[1])


def shards(
    mamba_inner,
    mamba_groups,
    selective_gate,
    step_raw,
    step_bias,
    decay_log,
    conv_inner,
    conv_groups,
    gated_norm_gain,
    query_rows,
    key_rows,
    value_rows,
    segment_ids,
    mamba_proj,
    attn_proj,
):
    item_count = segment_ids.shape[0]
    taps = conv_inner.shape[0]
    resident_heads = step_raw.shape[0]
    rim_inner, rim_groups, rim_marks = shifted(
        (
            mamba_inner[item_count - taps + 1 :],
            mamba_groups[item_count - taps + 1 :],
            segment_ids[item_count - taps + 1 :].astype(jnp.bfloat16),
        ),
        "seq",
        1,
    )
    rim_segs = rim_marks.astype(jnp.float32).astype(jnp.int32)
    prev_last = rim_segs[-1]
    inner_filtered = conv_silu(mamba_inner, conv_inner, segment_ids, rim_inner, rim_segs).reshape(
        item_count, resident_heads, HEAD_CHANNELS
    )
    groups_conv = conv_silu(mamba_groups, conv_groups, segment_ids, rim_groups, rim_segs)
    steps = jax.nn.softplus(step_raw + step_bias[:, None])
    rates = jnp.exp(decay_log)
    output, through, local_state, cumul = mamba_local(
        inner_filtered, groups_conv, segment_ids, steps, rates, prev_last
    )
    identity = (jnp.ones_like(through), jnp.zeros_like(local_state))
    carry_decay, carry_state = entering((through, local_state), "seq", combine_states, identity)
    selective_output = mamba_incoming(
        output, carry_state, groups_conv, segment_ids, cumul, prev_last
    )
    gated_values = selective_output * jax.nn.silu(selective_gate.astype(jnp.float32)).reshape(
        item_count, resident_heads, HEAD_CHANNELS
    )
    mean_square = jnp.mean(gated_values * gated_values, axis=-1, keepdims=True)
    normalized_rows = (
        (
            gated_values
            * lax.rsqrt(mean_square + 1e-05)
            * gated_norm_gain.reshape(resident_heads, HEAD_CHANNELS)
        )
        .astype(jnp.bfloat16)
        .reshape(item_count, resident_heads * HEAD_CHANNELS)
    )
    heads_here = query_rows.shape[1] // HD
    group_size = QH // KVH
    kv_index = lax.axis_index("head") * heads_here // group_size
    my_keys = lax.dynamic_slice_in_dim(key_rows, kv_index * HD, HD, 1)
    my_values = lax.dynamic_slice_in_dim(value_rows, kv_index * HD, HD, 1)
    marks = segment_ids.astype(jnp.bfloat16)
    block_start = lax.axis_index("seq") * item_count
    query_pos = block_start + jnp.arange(item_count, dtype=jnp.int32)
    queries = query_rows.reshape(item_count, heads_here, HD).transpose(1, 0, 2)
    scale = 1.0 / math.sqrt(HD)
    start_state = (
        jnp.full((heads_here, item_count), -1e30, jnp.float32),
        jnp.zeros((heads_here, item_count), jnp.float32),
        jnp.zeros((heads_here, item_count, HD), jnp.float32),
    )
    piece_keys = lax.all_gather(my_keys, "seq", axis=0, tiled=True)
    piece_values = lax.all_gather(my_values, "seq", axis=0, tiled=True)
    piece_marks = lax.all_gather(marks, "seq", axis=0, tiled=True)
    rows = piece_keys.shape[0]
    width = math.gcd(rows, item_count)
    blocks = rows // width

    def one_block(state, item):
        top, total, summed = state
        block_keys, block_values, block_marks, offset = item
        key_pos = offset * width + jnp.arange(width, dtype=jnp.int32)
        key_seg = block_marks.astype(jnp.float32).astype(jnp.int32)
        allowed = (
            (key_seg[None, :] == segment_ids[:, None])
            & (key_pos[None, :] <= query_pos[:, None])
            & (key_pos[None, :] >= 0)
        )
        scores = (
            jnp.einsum("hqd,kd->hqk", queries, block_keys, preferred_element_type=jnp.float32)
            * scale
        )
        scores = jnp.where(allowed[None], scores, -jnp.inf)
        new_top = jnp.maximum(top, jnp.max(scores, axis=-1))
        rescale = jnp.exp(top - new_top)
        weights = jnp.exp(scores - new_top[..., None])
        total = total * rescale + jnp.sum(weights, axis=-1)
        summed = summed * rescale[..., None] + jnp.einsum(
            "hqk,kd->hqd",
            weights.astype(jnp.bfloat16),
            block_values,
            preferred_element_type=jnp.float32,
        )
        return ((new_top, total, summed), None)

    items = (
        piece_keys.reshape(blocks, width, HD),
        piece_values.reshape(blocks, width, HD),
        piece_marks.reshape(blocks, width),
        jnp.arange(blocks, dtype=jnp.int32),
    )
    result, unused = lax.scan(one_block, start_state, items)
    top_final, total_final, summed_final = result
    attended = (
        (summed_final / total_final[..., None])
        .astype(jnp.bfloat16)
        .transpose(1, 0, 2)
        .reshape(item_count, heads_here * HD)
    )
    terms = jnp.dot(normalized_rows, mamba_proj, preferred_element_type=jnp.float32) + jnp.dot(
        attended, attn_proj, preferred_element_type=jnp.float32
    )
    return lax.psum_scatter(terms.astype(jnp.bfloat16), "head", scatter_dimension=1, tiled=True)


def solution(mesh):
    placed = (
        P("seq", "head"),
        P("seq", None),
        P("seq", "head"),
        P("head", "seq"),
        P("head"),
        P("head"),
        P(None, "head"),
        P(),
        P("head"),
        P("seq", "head"),
        P("seq", None),
        P("seq", None),
        P("seq"),
        P("head", None),
        P("head", None),
    )
    return jax.shard_map(
        shards, mesh=mesh, in_specs=placed, out_specs=P("seq", "head"), check_vma=False
    )
```

profile of v0, /device:TPU:0, one launch (start us, length us, event | category | flops | bytes accessed | tf_op | source)
XLA Modules:
  0.0 241.9 jit_solution(1705443980735956197)
XLA Ops:
  7.9 5.4 %collective-permute-start.1 = (bf16[3]{0:T(256)(128)(2,1)}, bf16[3]{0:T(256)(128)(2,1)}, u32[]{:S(2)}, u32[]{:S(2)}) collective-permute-start(bf16[3]{0:T(256)(128)(2,1)} %slice.85), channel_id=1, source_target_pairs={{0,4},{4,8},{8,12},{12,16},{16,20},{20,24},{24,28},{1,5},{5,9},{9,... | collective-permute-start | bytes 26 | tf_op jit(solution)/shard_map/ppermute | solution.py:17
  14.0 3.5 %collective-permute-start.2 = (bf16[3,512]{1,0:T(4,128)(2,1)S(1)}, bf16[3,512]{1,0:T(4,128)(2,1)}, u32[]{:S(2)}, u32[]{:S(2)}) collective-permute-start(bf16[3,512]{1,0:T(4,128)(2,1)S(1)} %slice.95), channel_id=1, source_target_pairs={{0,4},{4,8},{8,12},{12,16},{16,20},{20,24},{24,28},{1,5},{5,9},{9,... | collective-permute-start | bytes 9224 | tf_op jit(solution)/shard_map/ppermute | solution.py:17
  19.1 3.5 %collective-permute-start = (bf16[3,768]{0,1:T(8,128)(2,1)}, bf16[3,768]{0,1:T(8,128)(2,1)}, u32[]{:S(2)}, u32[]{:S(2)}) collective-permute-start(bf16[3,768]{0,1:T(8,128)(2,1)} %copy.27), channel_id=1, source_target_pairs={{0,4},{4,8},{8,12},{12,16},{16,20},{20,24},{24,28},{1,5},{5,9},{9,... | collective-permute-start | bytes 13832 | tf_op jit(solution)/shard_map/ppermute | solution.py:17
  22.6 1.2 slice.106
  23.8 1.6 convert_element_type.131
  25.5 1.1 copy.28
  31.8 32.9 %all_gather.23 = bf16[1024,128]{1,0:T(8,128)(2,1)} all-gather(bf16[128,128]{1,0:T(8,128)(2,1)S(1)} %constant_dynamic-slice_fusion.2), channel_id=1, replica_groups=mesh['seq'=8,'head'=4] {'seq'}, dimensions={0}, use_global_device_ids=true | all-gather | bytes 294912 | tf_op jit(solution)/shard_map/all_gather | solution.py:159
  65.5 32.9 %all_gather.24 = bf16[1024,128]{1,0:T(8,128)(2,1)} all-gather(bf16[128,128]{1,0:T(8,128)(2,1)S(1)} %constant_dynamic-slice_fusion.1), channel_id=1, replica_groups=mesh['seq'=8,'head'=4] {'seq'}, dimensions={0}, use_global_device_ids=true | all-gather | bytes 294912 | tf_op jit(solution)/shard_map/all_gather | solution.py:160
  98.4 16.8 %all-gather.2 = bf16[8,1,128]{2,1,0:T(2,128)(2,1)S(1)} all-gather(bf16[1,1,128]{2,1,0:T(2,128)(2,1)S(1)} %get-tuple-element.295), channel_id=1, replica_groups=mesh['seq'=8,'head'=4] {'seq'}, dimensions={0}, use_global_device_ids=true | all-gather | bytes 2304 | tf_op jit(solution)/shard_map/all_gather | solution.py:161
  115.8 0.9 copy.30
  118.8 2.0 compare_convert_fusion.4
  122.1 1.6 multiply_convert_fusion.2
  123.7 1.0 convert_element_type.120
  124.7 2.5 %multiply_convert_fusion.1 = bf16[128,768]{0,1:T(8,128)(2,1)S(1)} fusion(f32[128,768]{0,1:T(8,128)} %convert_element_type.121, f32[3,768]{0,1:T(8,128)S(1)} %convert_element_type.120, f32[768]{0:T(1024)S(1)} %get-tuple-element.241, f32[128]{0:T(128)S(1)} %get-tuple-element.290, f32[768]{0:T(1024)S(1)} %get-tuple-element.242, f32[128]{0:T(128)S(1)} %get-tuple-element.291, ...), kind=kLoop, calls=%fused_computation.74 | loop fusion | flops 1769472 | bytes 612864 | tf_op jit(solution)/shard_map/convert_element_type | solution.py:52
  127.9 1.2 convolution_convert_fusion
  129.2 32.5 %while.30 = (s32[]{:T(128)}, f32[2,128]{1,0:T(2,128)S(1)}, f32[2,128]{1,0:T(2,128)S(1)}, f32[2,128,128]{2,1,0:T(8,128)S(1)}, bf16[8,128]{1,0:T(8,128)(2,1)}, /*i...) while((s32[]{:T(128)}, f32[2,128]{1,0:T(2,128)S(1)}, ...), condition=%wide.region_7.8_spmd.clone, body=%wide.region_4.7_spmd.clone.sunk | while | flops 17172484 | bytes 840889 | solution.py:199
  132.2 1.0 convolution_add_fusion.3
  135.3 0.9 fusion.97
  136.3 1.0 convolution_add_fusion.3
  139.3 0.9 fusion.97
  140.4 1.0 convolution_add_fusion.3
  143.4 0.9 fusion.97
  144.4 1.0 convolution_add_fusion.3
  148.5 1.0 convolution_add_fusion.3
  151.5 0.9 fusion.97
  152.5 1.0 convolution_add_fusion.3
  155.6 0.9 fusion.97
  156.6 1.0 convolution_add_fusion.3
  159.6 1.0 fusion.97
  160.7 1.0 convolution_add_fusion.3
  161.7 1.8 copy.29
  164.3 1.3 dynamic-slice
  166.4 1.8 convert_multiply_fusion
  168.2 2.6 %fusion.76 = f32[128,2048]{1,0:T(8,128)} fusion(bf16[128,256]{0,1:T(8,128)(2,1)S(1)} %bitcast.93, bf16[256,2048]{1,0:T(8,128)(2,1)} %param.33), kind=kOutput, calls=%fused_computation.132 | convolution fusion | flops 134217728 | bytes 2162688 | tf_op jit(solution)/shard_map/dot_general | solution.py:207
  172.5 18.7 %all-reduce = bf16[96]{0:T(256)(128)(2,1)S(1)} all-reduce(bf16[96]{0:T(256)(128)(2,1)S(1)} %dynamic-update-slice), channel_id=2, replica_groups=mesh['seq'=8,'head'=4] {'seq'}, use_global_device_ids=true, to_apply=%add | all-reduce | flops 96 | bytes 384
  191.4 18.2 %while.29 = (s32[]{:T(128)}, f32[12,64,256]{2,1,0:T(8,128)}, s32[]{:T(128)}, bf16[8,12]{1,0:T(8,128)(2,1)S(1)}, bf16[8,12,64,256]{3,2,1,0:T(8,128)(2,1)}, /*index=5*/s32[]{:T(128)}, s32[]{:T(128)}) while((s32[]{:T(128)}, f32[12,64,256]{2,1,0:T(8,128)}, s32[]{:T(128)}, bf16[8,12]{1,0:T(8,128)(2,1)S(1)}, ...), condition=%wide.region_2.3_spmd.clone, body=%wide.region_1.2_spmd.clone.sunk | while | flops 983056 | bytes 1966305 | solution.py:40
  191.5 2.1 fusion.92
  193.5 2.3 fusion.92
  195.8 2.3 fusion.92
  198.1 2.3 fusion.92
  200.4 2.3 fusion.92
  202.7 2.3 fusion.92
  205.0 2.3 fusion.92
  207.3 2.3 fusion.92
  209.6 1.7 convolution_multiply_fusion.1
  211.3 2.8 %multiply_reduce_fusion = (f32[128,12]{0,1:T(8,128)S(1)}, f32[128,12,64]{0,2,1:T(8,128)S(1)}) fusion(f32[128,12,64]{0,2,1:T(8,128)} %bitcast.92, f32[128,12,64]{0,2,1:T(8,128)S(1)} %convolution_multiply_fusion.1, f32[12,128]{1,0:T(8,128)S(1)} %reduce_window_sum.11, f32[128,128]{1,0:T(8,128)S(1)} %fusion.66, pred[128,128]{1,0:T(8,128)(4,1)S(1)} %fusion.64, ...), kind=kOutput, calls=%fused_computation.69 | convolution fusion | flops 152173056 | bytes 1476608 | tf_op jit(solution)/shard_map/htj,jhd->thd/dot_general | solution.py:66
  214.4 1.4 fusion.20
  215.8 19.3 %reduce-scatter.2.cloned.1.call-done = bf16[128,512]{1,0:T(8,128)(2,1)} async-done(((bf16[128,2048]{1,0:T(8,128)(2,1)}), bf16[128,512]{1,0:T(8,128)(2,1)}) %reduce-scatter.2.cloned.1.call-update) | async-done | bytes 131088 | tf_op jit(solution)/shard_map/reduce_scatter | solution.py:210
  (149 shorter events, 29.9 us)
Async XLA Ops:
  6.5 207.8 %copy-start = (bf16[768,2048]{1,0:T(8,128)(2,1)S(1)}, bf16[768,2048]{1,0:T(8,128)(2,1)}, u32[]{:S(2)}) copy-start(bf16[768,2048]{1,0:T(8,128)(2,1)} %param.32) | copy-start | bytes 9437188
  6.5 122.6 %copy-start.5 = (s32[128]{0:T(128)S(1)}, s32[128]{0:T(128)}, u32[]{:S(2)}) copy-start(s32[128]{0:T(128)} %param.31) | copy-start | bytes 1540
  6.5 184.9 %all-gather.5.cloned.1.call-start = ((), (), s32[]{:S(2)}) async-start(), calls=%async_computation.2 | async-start | bytes 3538944 | tf_op jit(solution)/shard_map/all_gather | solution.py:23
  7.9 108.9 %collective-permute-start.1 = (bf16[3]{0:T(256)(128)(2,1)}, bf16[3]{0:T(256)(128)(2,1)}, u32[]{:S(2)}, u32[]{:S(2)}) collective-permute-start(bf16[3]{0:T(256)(128)(2,1)} %slice.85), channel_id=1, source_target_pairs={{0,4},{4,8},{8,12},{12,16},{16,20},{20,24},{24,28},{1,5},{5,9},{9,... | collective-permute-start | bytes 26 | tf_op jit(solution)/shard_map/ppermute | solution.py:17
  14.0 107.4 %collective-permute-start.2 = (bf16[3,512]{1,0:T(4,128)(2,1)S(1)}, bf16[3,512]{1,0:T(4,128)(2,1)}, u32[]{:S(2)}, u32[]{:S(2)}) collective-permute-start(bf16[3,512]{1,0:T(4,128)(2,1)S(1)} %slice.95), channel_id=1, source_target_pairs={{0,4},{4,8},{8,12},{12,16},{16,20},{20,24},{24,28},{1,5},{5,9},{9,... | collective-permute-start | bytes 9224 | tf_op jit(solution)/shard_map/ppermute | solution.py:17
  19.1 104.6 %collective-permute-start = (bf16[3,768]{0,1:T(8,128)(2,1)}, bf16[3,768]{0,1:T(8,128)(2,1)}, u32[]{:S(2)}, u32[]{:S(2)}) collective-permute-start(bf16[3,768]{0,1:T(8,128)(2,1)} %copy.27), channel_id=1, source_target_pairs={{0,4},{4,8},{8,12},{12,16},{16,20},{20,24},{24,28},{1,5},{5,9},{9,... | collective-permute-start | bytes 13832 | tf_op jit(solution)/shard_map/ppermute | solution.py:17
  30.6 98.6 %copy-start.6 = (f32[128,12]{0,1:T(8,128)}, f32[128,12]{0,1:T(8,128)S(1)}, u32[]{:S(2)}) copy-start(f32[128,12]{0,1:T(8,128)S(1)} %get-tuple-element.281) | copy-start | bytes 18436
  123.7 3.5 %copy-start.2 = (bf16[128,512]{1,0:T(8,128)(2,1)}, bf16[128,512]{1,0:T(8,128)(2,1)S(1)}, u32[]{:S(2)}) copy-start(bf16[128,512]{1,0:T(8,128)(2,1)S(1)} %multiply_convert_fusion.2) | copy-start | bytes 393220
  127.2 0.7 copy-start.4
  127.2 36.3 %copy-start.10 = (f32[768]{0:T(1024)S(1)}, f32[768]{0:T(1024)}, u32[]{:S(2)}) copy-start(f32[768]{0:T(1024)} %param.27) | copy-start | bytes 9220
  129.1 106.0 %reduce-scatter.2.cloned.1.call-start = ((), (), s32[]{:S(2)}) async-start(), calls=%async_computation.1 | async-start | bytes 655360 | tf_op jit(solution)/shard_map/reduce_scatter | solution.py:210
  161.7 29.6 %copy-start.3 = (bf16[128,512]{1,0:T(8,128)(2,1)S(1)}, bf16[128,512]{1,0:T(8,128)(2,1)}, u32[]{:S(2)}) copy-start(bf16[128,512]{1,0:T(8,128)(2,1)} %copy-done.2) | copy-start | bytes 393220
  191.4 18.2 %copy-start.8 = (f32[128,12]{0,1:T(8,128)S(1)}, f32[128,12]{0,1:T(8,128)}, u32[]{:S(2)}) copy-start(f32[128,12]{0,1:T(8,128)} %get-tuple-element.283) | copy-start | bytes 18436
  191.4 19.9 %copy-start.7 = (f32[128,12]{0,1:T(8,128)S(1)}, f32[128,12]{0,1:T(8,128)}, u32[]{:S(2)}) copy-start(f32[128,12]{0,1:T(8,128)} %copy-done.6) | copy-start | bytes 18436
  191.4 22.7 %copy-start.9 = (f32[12,64]{1,0:T(8,128)S(1)}, f32[12,64]{1,0:T(8,128)}, u32[]{:S(2)}) copy-start(f32[12,64]{1,0:T(8,128)} %mul.345) | copy-start | bytes 9220
  209.6 4.7 %copy-start.1 = (f32[128,2048]{1,0:T(8,128)S(1)}, f32[128,2048]{1,0:T(8,128)}, u32[]{:S(2)}) copy-start(f32[128,2048]{1,0:T(8,128)} %fusion.76) | copy-start | bytes 3145732
Sparse Core Ops, SparseCore 0:
  129.2 58.6 all-gather.4
  215.9 19.1 reduce-scatter.1
where the time goes:
time: 244 us; the launch traced here: 242 us
  blocking collectives  101 us (41%)
  other arithmetic  41.5 us (17%)
  matrix products  25.3 us (10%)
  local copies, waits for them, and re-layouts  21.2 us (9%)
  waiting for transfers between devices  19.4 us (8%)
  between operations  15.7 us (6%)
  starting transfers between devices  12.4 us (5%)
  loops' own time  5.2 us (2%)
    all_gather x1, blocking collectives, shards(): piece_keys = lax.all_gather(my_keys, 'seq', axis=0, tiled=True)  32.9 us
    all_gather x1, blocking collectives, shards(): piece_values = lax.all_gather(my_values, 'seq', axis=0, tiled=True)  32.9 us
    reduce_scatter x1, waiting for transfers between devices, shards(): lax.psum_scatter(terms.astype(jnp.bfloat16), 'head', scatter_dimension=1,...  19.3 us
    unnamed x1, blocking collectives  18.7 us
    select_n x8, other arithmetic, turn(): return jax.tree.map(lambda a, b: jnp.where(reached, a, b), new, before)  18.1 us
    all_gather x1, blocking collectives, shards(): piece_marks = lax.all_gather(marks, 'seq', axis=0, tiled=True)  16.8 us
    ppermute x3, starting transfers between devices, shifted(): lax.ppermute(value, axis, [(source, source + steps) for source in range(f...  12.4 us
    dot_general x8, matrix products, one_block(): jnp.einsum('hqk,kd->hqd', weights.astype(jnp.bfloat16), block_values, pre...  7.87 us
  transfers between devices with their start and end apart: 5, of which 1 were waited for; matrix products, arithmetic and copies ran while one was open for 24% of the time, Pallas kernels for 0%

commit v1 on v0

--- a/solution.py
+++ b/solution.py
@@ -156,8 +156,17 @@
         jnp.zeros((heads_here, item_count), jnp.float32),
         jnp.zeros((heads_here, item_count, HD), jnp.float32),
     )
-    piece_keys = lax.all_gather(my_keys, "seq", axis=0, tiled=True)
-    piece_values = lax.all_gather(my_values, "seq", axis=0, tiled=True)
+
+    def cubes_handle(own_rows, local):
+        return jnp.split(
+            lax.all_gather(
+                jnp.concatenate([own_rows, local], axis=1), tiled=True, axis=0, axis_name="seq"
+            ),
+            [own_rows.shape[1]],
+            1,
+        )
+
+    piece_keys, piece_values = cubes_handle(my_keys, my_values)
     piece_marks = lax.all_gather(marks, "seq", axis=0, tiled=True)
     rows = piece_keys.shape[0]
     width = math.gcd(rows, item_count)

time: 244 us -> 209 us (0.86)
  blocking collectives: 101 us -> 66.9 us
    all_gather x2 -> x1, blocking collectives: 65.8 us -> 31.4 us  [cubes_handle(): lax.all_gather(jnp.concatenate([own_rows, local], axis=1), tiled=True, ax...]
  transfers between devices with their start and end apart: 5 -> 5, of which waited for: 1 -> 1; matrix products, arithmetic and copies ran while one was open for 24% -> 27% of each run, Pallas kernels for 0% -> 0%
where the time goes in v1:
time: 209 us; the launch traced here: 207 us
  blocking collectives  66.9 us (32%)
  other arithmetic  40.2 us (19%)
  matrix products  25.3 us (12%)
  local copies, waits for them, and re-layouts  21.3 us (10%)
  waiting for transfers between devices  19.7 us (9%)
  between operations  15.7 us (8%)
  starting transfers between devices  12.4 us (6%)
  loops' own time  5.2 us (2%)
    all_gather x1, blocking collectives, cubes_handle(): lax.all_gather(jnp.concatenate([own_rows, local], axis=1), tiled=True, ax...  31.4 us
    reduce_scatter x1, waiting for transfers between devices, shards(): lax.psum_scatter(terms.astype(jnp.bfloat16), 'head', scatter_dimension=1,...  19.6 us
    unnamed x1, blocking collectives  18.3 us
    select_n x8, other arithmetic, turn(): return jax.tree.map(lambda a, b: jnp.where(reached, a, b), new, before)  18.1 us
    all_gather x1, blocking collectives, shards(): piece_marks = lax.all_gather(marks, 'seq', axis=0, tiled=True)  17.1 us
    ppermute x3, starting transfers between devices, shifted(): lax.ppermute(value, axis, [(source, source + steps) for source in range(f...  12.4 us
    dot_general x8, matrix products, one_block(): jnp.einsum('hqk,kd->hqd', weights.astype(jnp.bfloat16), block_values, pre...  7.86 us
    dot_general x8, matrix products, one_block(): jnp.einsum('hqd,kd->hqk', queries, block_keys, preferred_element_type=jnp...  7.61 us
  transfers between devices with their start and end apart: 5, of which 1 were waited for; matrix products, arithmetic and copies ran while one was open for 27% of the time, Pallas kernels for 0%

profile of v1, /device:TPU:0, one launch (start us, length us, event | category | flops | bytes accessed | tf_op | source)
XLA Modules:
  0.0 206.6 jit_solution(13640407440944146876)
XLA Ops:
  7.9 5.4 %collective-permute-start.1 = (bf16[3]{0:T(256)(128)(2,1)}, bf16[3]{0:T(256)(128)(2,1)}, u32[]{:S(2)}, u32[]{:S(2)}) collective-permute-start(bf16[3]{0:T(256)(128)(2,1)} %slice.85), channel_id=1, source_target_pairs={{0,4},{4,8},{8,12},{12,16},{16,20},{20,24},{24,28},{1,5},{5,9},{9,... | collective-permute-start | bytes 26 | tf_op jit(solution)/shard_map/ppermute | solution.py:17
  14.0 3.5 %collective-permute-start.2 = (bf16[3,512]{1,0:T(4,128)(2,1)S(1)}, bf16[3,512]{1,0:T(4,128)(2,1)}, u32[]{:S(2)}, u32[]{:S(2)}) collective-permute-start(bf16[3,512]{1,0:T(4,128)(2,1)S(1)} %slice.95), channel_id=1, source_target_pairs={{0,4},{4,8},{8,12},{12,16},{16,20},{20,24},{24,28},{1,5},{5,9},{9,... | collective-permute-start | bytes 9224 | tf_op jit(solution)/shard_map/ppermute | solution.py:17
  19.1 3.5 %collective-permute-start = (bf16[3,768]{0,1:T(8,128)(2,1)}, bf16[3,768]{0,1:T(8,128)(2,1)}, u32[]{:S(2)}, u32[]{:S(2)}) collective-permute-start(bf16[3,768]{0,1:T(8,128)(2,1)} %copy.27), channel_id=1, source_target_pairs={{0,4},{4,8},{8,12},{12,16},{16,20},{20,24},{24,28},{1,5},{5,9},{9,... | collective-permute-start | bytes 13832 | tf_op jit(solution)/shard_map/ppermute | solution.py:17
  22.6 1.2 slice.106
  23.8 1.6 convert_element_type.131
  25.5 1.1 copy.28
  31.9 31.4 %all_gather.20 = bf16[1024,256]{1,0:T(8,128)(2,1)S(1)} all-gather(bf16[128,256]{1,0:T(8,128)(2,1)S(1)} %pad_maximum_fusion.2), channel_id=1, replica_groups=mesh['seq'=8,'head'=4] {'seq'}, dimensions={0}, use_global_device_ids=true | all-gather | bytes 589824 | tf_op jit(solution)/shard_map/all_gather | solution.py:162
  64.1 17.1 %all-gather.2 = bf16[8,1,128]{2,1,0:T(2,128)(2,1)S(1)} all-gather(bf16[1,1,128]{2,1,0:T(2,128)(2,1)S(1)} %get-tuple-element.297), channel_id=1, replica_groups=mesh['seq'=8,'head'=4] {'seq'}, dimensions={0}, use_global_device_ids=true | all-gather | bytes 2304 | tf_op jit(solution)/shard_map/all_gather | solution.py:170
  81.8 0.9 copy.30
  84.2 1.3 compare_convert_fusion.4
  86.8 1.6 multiply_convert_fusion.2
  88.4 1.0 convert_element_type.120
  89.4 2.5 %multiply_convert_fusion.1 = bf16[128,768]{0,1:T(8,128)(2,1)S(1)} fusion(f32[128,768]{0,1:T(8,128)} %convert_element_type.121, f32[3,768]{0,1:T(8,128)S(1)} %convert_element_type.120, f32[768]{0:T(1024)S(1)} %get-tuple-element.241, f32[128]{0:T(128)S(1)} %get-tuple-element.292, f32[768]{0:T(1024)S(1)} %get-tuple-element.242, f32[128]{0:T(128)S(1)} %get-tuple-element.293, ...), kind=kLoop, calls=%fused_computation.74 | loop fusion | flops 1769472 | bytes 612864 | tf_op jit(solution)/shard_map/convert_element_type | solution.py:52
  92.6 1.2 convolution_convert_fusion
  93.9 32.5 %while.30 = (s32[]{:T(128)}, f32[2,128]{1,0:T(2,128)S(1)}, f32[2,128]{1,0:T(2,128)S(1)}, f32[2,128,128]{2,1,0:T(8,128)S(1)}, bf16[8,128]{1,0:T(8,128)(2,1)}, /*i...) while((s32[]{:T(128)}, f32[2,128]{1,0:T(2,128)S(1)}, ...), condition=%wide.region_7.8_spmd.clone, body=%wide.region_4.7_spmd.clone.sunk | while | flops 17172484 | bytes 840889 | solution.py:208
  95.9 1.0 fusion.98
  97.0 1.0 convolution_add_fusion.3
  100.0 1.0 fusion.98
  101.0 1.0 convolution_add_fusion.3
  104.1 0.9 fusion.98
  105.1 1.0 convolution_add_fusion.3
  108.1 0.9 fusion.98
  109.2 1.0 convolution_add_fusion.3
  112.2 0.9 fusion.98
  113.2 1.0 convolution_add_fusion.3
  116.2 1.0 fusion.98
  117.3 1.0 convolution_add_fusion.3
  120.3 1.0 fusion.98
  121.3 1.0 convolution_add_fusion.3
  125.4 1.0 convolution_add_fusion.3
  126.4 1.8 copy.29
  129.0 1.3 dynamic-slice
  131.1 1.8 convert_multiply_fusion
  132.9 2.5 %fusion.77 = f32[128,2048]{1,0:T(8,128)} fusion(bf16[128,256]{0,1:T(8,128)(2,1)S(1)} %bitcast.93, bf16[256,2048]{1,0:T(8,128)(2,1)} %param.33), kind=kOutput, calls=%fused_computation.134 | convolution fusion | flops 134217728 | bytes 2162688 | tf_op jit(solution)/shard_map/dot_general | solution.py:216
  137.2 18.3 %all-reduce = bf16[96]{0:T(256)(128)(2,1)S(1)} all-reduce(bf16[96]{0:T(256)(128)(2,1)S(1)} %dynamic-update-slice), channel_id=2, replica_groups=mesh['seq'=8,'head'=4] {'seq'}, use_global_device_ids=true, to_apply=%add | all-reduce | flops 96 | bytes 384
  155.8 18.2 %while.29 = (s32[]{:T(128)}, f32[12,64,256]{2,1,0:T(8,128)}, s32[]{:T(128)}, bf16[8,12]{1,0:T(8,128)(2,1)S(1)}, bf16[8,12,64,256]{3,2,1,0:T(8,128)(2,1)}, /*index=5*/s32[]{:T(128)}, s32[]{:T(128)}) while((s32[]{:T(128)}, f32[12,64,256]{2,1,0:T(8,128)}, s32[]{:T(128)}, bf16[8,12]{1,0:T(8,128)(2,1)S(1)}, ...), condition=%wide.region_2.3_spmd.clone, body=%wide.region_1.2_spmd.clone.sunk | while | flops 983056 | bytes 1966305 | solution.py:40
  155.8 2.1 fusion.93
  157.9 2.3 %fusion.93 = f32[12,64,256]{2,1,0:T(8,128)} fusion(f32[12,64,256]{2,1,0:T(8,128)} %get-tuple-element.462, bf16[8,12,64,256]{3,2,1,0:T(8,128)(2,1)} %get-tuple-element.472, s32[]{:T(128)} %get-tuple-element.461, f32[12]{0:T(128)S(1)} %bitcast_convert_fusion.2, pred[]{:T(512)S(6)} %compare.8, pred[]{:T(512)S(6)} %lt.32), kind=kLoop, calls=%fused_computation.2.clone.1 | loop fusion | flops 983040 | bytes 1966134 | tf_op jit(solution)/shard_map/while/body/eval_jaxpr/jit(_where)/select_n | solution.py:38
  160.2 2.3 %fusion.93 = f32[12,64,256]{2,1,0:T(8,128)} fusion(f32[12,64,256]{2,1,0:T(8,128)} %get-tuple-element.462, bf16[8,12,64,256]{3,2,1,0:T(8,128)(2,1)} %get-tuple-element.472, s32[]{:T(128)} %get-tuple-element.461, f32[12]{0:T(128)S(1)} %bitcast_convert_fusion.2, pred[]{:T(512)S(6)} %compare.8, pred[]{:T(512)S(6)} %lt.32), kind=kLoop, calls=%fused_computation.2.clone.1 | loop fusion | flops 983040 | bytes 1966134 | tf_op jit(solution)/shard_map/while/body/eval_jaxpr/jit(_where)/select_n | solution.py:38
  162.5 2.3 %fusion.93 = f32[12,64,256]{2,1,0:T(8,128)} fusion(f32[12,64,256]{2,1,0:T(8,128)} %get-tuple-element.462, bf16[8,12,64,256]{3,2,1,0:T(8,128)(2,1)} %get-tuple-element.472, s32[]{:T(128)} %get-tuple-element.461, f32[12]{0:T(128)S(1)} %bitcast_convert_fusion.2, pred[]{:T(512)S(6)} %compare.8, pred[]{:T(512)S(6)} %lt.32), kind=kLoop, calls=%fused_computation.2.clone.1 | loop fusion | flops 983040 | bytes 1966134 | tf_op jit(solution)/shard_map/while/body/eval_jaxpr/jit(_where)/select_n | solution.py:38
  164.8 2.3 %fusion.93 = f32[12,64,256]{2,1,0:T(8,128)} fusion(f32[12,64,256]{2,1,0:T(8,128)} %get-tuple-element.462, bf16[8,12,64,256]{3,2,1,0:T(8,128)(2,1)} %get-tuple-element.472, s32[]{:T(128)} %get-tuple-element.461, f32[12]{0:T(128)S(1)} %bitcast_convert_fusion.2, pred[]{:T(512)S(6)} %compare.8, pred[]{:T(512)S(6)} %lt.32), kind=kLoop, calls=%fused_computation.2.clone.1 | loop fusion | flops 983040 | bytes 1966134 | tf_op jit(solution)/shard_map/while/body/eval_jaxpr/jit(_where)/select_n | solution.py:38
  167.1 2.3 %fusion.93 = f32[12,64,256]{2,1,0:T(8,128)} fusion(f32[12,64,256]{2,1,0:T(8,128)} %get-tuple-element.462, bf16[8,12,64,256]{3,2,1,0:T(8,128)(2,1)} %get-tuple-element.472, s32[]{:T(128)} %get-tuple-element.461, f32[12]{0:T(128)S(1)} %bitcast_convert_fusion.2, pred[]{:T(512)S(6)} %compare.8, pred[]{:T(512)S(6)} %lt.32), kind=kLoop, calls=%fused_computation.2.clone.1 | loop fusion | flops 983040 | bytes 1966134 | tf_op jit(solution)/shard_map/while/body/eval_jaxpr/jit(_where)/select_n | solution.py:38
  169.4 2.3 %fusion.93 = f32[12,64,256]{2,1,0:T(8,128)} fusion(f32[12,64,256]{2,1,0:T(8,128)} %get-tuple-element.462, bf16[8,12,64,256]{3,2,1,0:T(8,128)(2,1)} %get-tuple-element.472, s32[]{:T(128)} %get-tuple-element.461, f32[12]{0:T(128)S(1)} %bitcast_convert_fusion.2, pred[]{:T(512)S(6)} %compare.8, pred[]{:T(512)S(6)} %lt.32), kind=kLoop, calls=%fused_computation.2.clone.1 | loop fusion | flops 983040 | bytes 1966134 | tf_op jit(solution)/shard_map/while/body/eval_jaxpr/jit(_where)/select_n | solution.py:38
  171.7 2.3 %fusion.93 = f32[12,64,256]{2,1,0:T(8,128)} fusion(f32[12,64,256]{2,1,0:T(8,128)} %get-tuple-element.462, bf16[8,12,64,256]{3,2,1,0:T(8,128)(2,1)} %get-tuple-element.472, s32[]{:T(128)} %get-tuple-element.461, f32[12]{0:T(128)S(1)} %bitcast_convert_fusion.2, pred[]{:T(512)S(6)} %compare.8, pred[]{:T(512)S(6)} %lt.32), kind=kLoop, calls=%fused_computation.2.clone.1 | loop fusion | flops 983040 | bytes 1966134 | tf_op jit(solution)/shard_map/while/body/eval_jaxpr/jit(_where)/select_n | solution.py:38
  174.0 1.7 convolution_multiply_fusion.1
  175.7 2.8 %multiply_reduce_fusion = (f32[128,12]{0,1:T(8,128)S(1)}, f32[128,12,64]{0,2,1:T(8,128)S(1)}) fusion(f32[128,12,64]{0,2,1:T(8,128)} %bitcast.92, f32[128,12,64]{0,2,1:T(8,128)S(1)} %convolution_multiply_fusion.1, f32[12,128]{1,0:T(8,128)S(1)} %reduce_window_sum.11, f32[128,128]{1,0:T(8,128)S(1)} %fusion.66, pred[128,128]{1,0:T(8,128)(4,1)S(1)} %fusion.64, ...), kind=kOutput, calls=%fused_computation.69 | convolution fusion | flops 152173056 | bytes 1476608 | tf_op jit(solution)/shard_map/htj,jhd->thd/dot_general | solution.py:66
  178.7 1.4 fusion.20
  180.1 19.6 %reduce-scatter.2.cloned.1.call-done = bf16[128,512]{1,0:T(8,128)(2,1)} async-done(((bf16[128,2048]{1,0:T(8,128)(2,1)}), bf16[128,512]{1,0:T(8,128)(2,1)}) %reduce-scatter.2.cloned.1.call-update) | async-done | bytes 131088 | tf_op jit(solution)/shard_map/reduce_scatter | solution.py:219
  (149 shorter events, 28.3 us)
Async XLA Ops:
  6.5 172.2 %copy-start = (bf16[768,2048]{1,0:T(8,128)(2,1)S(1)}, bf16[768,2048]{1,0:T(8,128)(2,1)}, u32[]{:S(2)}) copy-start(bf16[768,2048]{1,0:T(8,128)(2,1)} %param.32) | copy-start | bytes 9437188
  6.5 77.6 %copy-start.5 = (s32[128]{0:T(128)S(1)}, s32[128]{0:T(128)}, u32[]{:S(2)}) copy-start(s32[128]{0:T(128)} %param.31) | copy-start | bytes 1540
  6.5 149.2 %all-gather.5.cloned.1.call-start = ((), (), s32[]{:S(2)}) async-start(), calls=%async_computation.2 | async-start | bytes 3538944 | tf_op jit(solution)/shard_map/all_gather | solution.py:23
  7.9 74.9 %collective-permute-start.1 = (bf16[3]{0:T(256)(128)(2,1)}, bf16[3]{0:T(256)(128)(2,1)}, u32[]{:S(2)}, u32[]{:S(2)}) collective-permute-start(bf16[3]{0:T(256)(128)(2,1)} %slice.85), channel_id=1, source_target_pairs={{0,4},{4,8},{8,12},{12,16},{16,20},{20,24},{24,28},{1,5},{5,9},{9,... | collective-permute-start | bytes 26 | tf_op jit(solution)/shard_map/ppermute | solution.py:17
  14.0 72.1 %collective-permute-start.2 = (bf16[3,512]{1,0:T(4,128)(2,1)S(1)}, bf16[3,512]{1,0:T(4,128)(2,1)}, u32[]{:S(2)}, u32[]{:S(2)}) collective-permute-start(bf16[3,512]{1,0:T(4,128)(2,1)S(1)} %slice.95), channel_id=1, source_target_pairs={{0,4},{4,8},{8,12},{12,16},{16,20},{20,24},{24,28},{1,5},{5,9},{9,... | collective-permute-start | bytes 9224 | tf_op jit(solution)/shard_map/ppermute | solution.py:17
  19.1 69.3 %collective-permute-start = (bf16[3,768]{0,1:T(8,128)(2,1)}, bf16[3,768]{0,1:T(8,128)(2,1)}, u32[]{:S(2)}, u32[]{:S(2)}) collective-permute-start(bf16[3,768]{0,1:T(8,128)(2,1)} %copy.27), channel_id=1, source_target_pairs={{0,4},{4,8},{8,12},{12,16},{16,20},{20,24},{24,28},{1,5},{5,9},{9,... | collective-permute-start | bytes 13832 | tf_op jit(solution)/shard_map/ppermute | solution.py:17
  30.6 63.3 %copy-start.6 = (f32[128,12]{0,1:T(8,128)}, f32[128,12]{0,1:T(8,128)S(1)}, u32[]{:S(2)}) copy-start(f32[128,12]{0,1:T(8,128)S(1)} %get-tuple-element.283) | copy-start | bytes 18436
  88.4 3.5 %copy-start.2 = (bf16[128,512]{1,0:T(8,128)(2,1)}, bf16[128,512]{1,0:T(8,128)(2,1)S(1)}, u32[]{:S(2)}) copy-start(bf16[128,512]{1,0:T(8,128)(2,1)S(1)} %multiply_convert_fusion.2) | copy-start | bytes 393220
  91.9 0.7 copy-start.4
  91.9 36.3 %copy-start.10 = (f32[768]{0:T(1024)S(1)}, f32[768]{0:T(1024)}, u32[]{:S(2)}) copy-start(f32[768]{0:T(1024)} %param.27) | copy-start | bytes 9220
  93.8 105.9 %reduce-scatter.2.cloned.1.call-start = ((), (), s32[]{:S(2)}) async-start(), calls=%async_computation.1 | async-start | bytes 655360 | tf_op jit(solution)/shard_map/reduce_scatter | solution.py:219
  126.4 29.2 %copy-start.3 = (bf16[128,512]{1,0:T(8,128)(2,1)S(1)}, bf16[128,512]{1,0:T(8,128)(2,1)}, u32[]{:S(2)}) copy-start(bf16[128,512]{1,0:T(8,128)(2,1)} %copy-done.2) | copy-start | bytes 393220
  155.8 18.2 %copy-start.8 = (f32[128,12]{0,1:T(8,128)S(1)}, f32[128,12]{0,1:T(8,128)}, u32[]{:S(2)}) copy-start(f32[128,12]{0,1:T(8,128)} %get-tuple-element.285) | copy-start | bytes 18436
  155.8 19.9 %copy-start.7 = (f32[128,12]{0,1:T(8,128)S(1)}, f32[128,12]{0,1:T(8,128)}, u32[]{:S(2)}) copy-start(f32[128,12]{0,1:T(8,128)} %copy-done.6) | copy-start | bytes 18436
  155.8 22.7 %copy-start.9 = (f32[12,64]{1,0:T(8,128)S(1)}, f32[12,64]{1,0:T(8,128)}, u32[]{:S(2)}) copy-start(f32[12,64]{1,0:T(8,128)} %mul.345) | copy-start | bytes 9220
  174.0 4.7 %copy-start.1 = (f32[128,2048]{1,0:T(8,128)S(1)}, f32[128,2048]{1,0:T(8,128)}, u32[]{:S(2)}) copy-start(f32[128,2048]{1,0:T(8,128)} %fusion.77) | copy-start | bytes 3145732
Sparse Core Ops, SparseCore 0:
  94.0 58.4 all-gather.4
  180.3 19.4 reduce-scatter.1
